TPU v7x, 32 devices: a whole 2x2x4 slice. The times are simulated.
32 devices in a mesh: row: 4 (over y, x), col: 8 (over z, core).
Axes of the slice: x: 2, y: 2, z: 4, core: 2. Of those that a mesh axis runs over, the one named last changes fastest.
Arguments:
- z_slab: float32 [1024, 1024], P('col', 'row'), may hold values from -6 to 6
- prev_factor: bfloat16 [1024, 32768], P('row', 'col'), may hold values from -0.03125 to 0.03125
- prev_solution: bfloat16 [1024, 32768], P(None, 'col'), may hold values from -6 to 6
- slab_factor: bfloat16 [1024, 1024], P('row'), may hold values from -0.09375 to 0.09375
- diag_inverse: bfloat16 [1024, 256], P('row'), may hold values from -1 to 2, as said below
Outputs:
- solved: float32 [1024, 1024], P('col', 'row')
Inputs may be any that keep to these rules, and one draw needn't show every extreme that they name: `diag_inverse`: each 256 x 256 block is lower triangular with its diagonal between 1 and 2.
All inputs are finite; a program needn't handle non-finite values.
Results may differ from a plain program's by a relative error of at most 0.0003.
Values sent between devices are 32-bit elements; how exact they have to be, the bound alone decides.
A program may use at most 64 MiB of HBM per device.

v0:
```python
import jax
import jax.numpy as jnp
from jax import lax
from jax.sharding import PartitionSpec as P


def spread(block, axis, owner):
    block = jnp.where(lax.axis_index(axis) == owner, block, jnp.zeros_like(block))
    return lax.psum(block, axis)


def precise_dot(left, right):
    return lax.dot_general(
        left,
        right,
        (((1,), (1,)), ((), ())),
        precision=lax.Precision.HIGHEST,
        preferred_element_type=jnp.float32,
    )


def on_device(z_slab, prev_factor, prev_solution, slab_factor, diag_inverse):
    row_count = z_slab.shape[0]
    block_width = diag_inverse.shape[1]
    block_rows = lax.axis_size("row")
    partial_value = lax.dot_general(
        prev_solution, prev_factor, (((1,), (1,)), ((), ())), preferred_element_type=jnp.float32
    )
    summed = lax.psum(partial_value, "col")
    fan_sum = lax.dynamic_slice_in_dim(summed, lax.axis_index("col") * row_count, row_count, 0)
    remainder = z_slab - fan_sum
    factor = slab_factor.astype(jnp.float32)
    inverse = diag_inverse.astype(jnp.float32)
    device_row = lax.axis_index("row")
    result = jnp.zeros((row_count, block_width), jnp.float32)
    updates = jnp.zeros((row_count, block_width), jnp.float32)

    def bcast_step(block_index, carry):
        result, updates = carry
        candidate = precise_dot(remainder - updates, inverse)
        arrived = spread(candidate, "row", block_index)
        result = jnp.where(device_row == block_index, arrived, result)
        columns = lax.dynamic_slice_in_dim(factor, block_index * block_width, block_width, 1)
        updates = updates + precise_dot(arrived, columns)
        return (result, updates)

    result, updates = lax.fori_loop(0, block_rows, bcast_step, (result, updates))
    return result


def solution(mesh):
    in_specs = (P("col", "row"), P("row", "col"), P(None, "col"), P("row", None), P("row", None))
    out_specs = P("col", "row")
    return jax.shard_map(
        on_device, mesh=mesh, in_specs=in_specs, out_specs=out_specs, check_vma=False
    )
```

profile of v0, /device:TPU:14, one launch (start us, length us, event | category | flops | bytes accessed | tf_op | source)
XLA Modules:
  0.0 274.6 jit_solution(165684188814202454)
XLA Ops:
  6.5 0.0 copy-start
  6.5 0.0 all-reduce.3.cloned.1.call-start
  6.5 1.6 copy-done
  8.1 6.8 %fusion.7 = f32[1024,256]{1,0:T(8,128)} fusion(bf16[1024,4096]{1,0:T(8,128)(2,1)} %param.9, bf16[256,4096]{1,0:T(8,128)(2,1)S(1)} %copy-done), kind=kOutput, calls=%fused_computation.11 | convolution fusion | flops 2147483648 | bytes 11534336 | tf_op jit(solution)/shard_map/dot_general | solution.py:26
  14.9 0.0 all-reduce.3.cloned.1.call-update
  15.0 1.1 convert_element_type.7
  16.1 0.9 convert_element_type.6
  17.0 57.2 %all-reduce.3.cloned.1.call-done = f32[1024,256]{1,0:T(8,128)} async-done(((f32[1024,256]{1,0:T(8,128)}), f32[1024,256]{1,0:T(8,128)}) %all-reduce.3.cloned.1.call-update) | async-done | bytes 1048592 | tf_op jit(solution)/shard_map/psum | solution.py:29
  74.2 1.6 dynamic-slice_subtract_fusion
  75.8 192.3 %while.16 = (s32[]{:T(128)}, f32[128,256]{1,0:T(8,128)}, f32[128,256]{1,0:T(8,128)S(1)}, s32[]{:T(128)}, f32[128,256]{1,0:T(8,128)}, /*index=5*/f32[256,256]{1,0...) while((s32[]{:T(128)}, f32[128,256]{1,0:T(8,128)}, ...), condition=%wide.region_3.4_spmd.clone, body=%wide.region_1.3_spmd.clone.sunk | while | flops 201588736 | bytes 2490639 | solution.py:47
  75.8 0.0 all-reduce.5.cloned.1.call-start
  75.8 1.9 convolution_select_fusion.2
  77.8 0.0 all-reduce.5.cloned.1.call-update
  77.8 42.6 %all-reduce.5.cloned.1.call-done = f32[128,256]{1,0:T(8,128)} async-done(((f32[128,256]{1,0:T(8,128)}), f32[128,256]{1,0:T(8,128)}) %all-reduce.5.cloned.1.call-update) | async-done | bytes 131088 | tf_op jit(solution)/shard_map/while/body/eval_jaxpr/psum | solution.py:9
  120.4 1.4 convolution_add_fusion.2
  121.8 0.7 select_select_fusion.2
  122.5 0.0 all-reduce.5.cloned.1.call-start
  122.5 2.0 convolution_select_fusion.2
  124.4 0.0 all-reduce.5.cloned.1.call-update
  124.5 43.8 %all-reduce.5.cloned.1.call-done = f32[128,256]{1,0:T(8,128)} async-done(((f32[128,256]{1,0:T(8,128)}), f32[128,256]{1,0:T(8,128)}) %all-reduce.5.cloned.1.call-update) | async-done | bytes 131088 | tf_op jit(solution)/shard_map/while/body/eval_jaxpr/psum | solution.py:9
  168.2 1.4 convolution_add_fusion.2
  169.6 1.6 select_select_fusion.2
  171.2 0.0 all-reduce.5.cloned.1.call-start
  171.2 1.9 convolution_select_fusion.2
  173.2 0.0 all-reduce.5.cloned.1.call-update
  173.2 43.5 %all-reduce.5.cloned.1.call-done = f32[128,256]{1,0:T(8,128)} async-done(((f32[128,256]{1,0:T(8,128)}), f32[128,256]{1,0:T(8,128)}) %all-reduce.5.cloned.1.call-update) | async-done | bytes 131088 | tf_op jit(solution)/shard_map/while/body/eval_jaxpr/psum | solution.py:9
  216.7 1.4 convolution_add_fusion.2
  218.1 1.6 select_select_fusion.2
  219.7 0.0 all-reduce.5.cloned.1.call-start
  219.7 2.0 convolution_select_fusion.2
  221.6 0.0 all-reduce.5.cloned.1.call-update
  221.6 43.4 %all-reduce.5.cloned.1.call-done = f32[128,256]{1,0:T(8,128)} async-done(((f32[128,256]{1,0:T(8,128)}), f32[128,256]{1,0:T(8,128)}) %all-reduce.5.cloned.1.call-update) | async-done | bytes 131088 | tf_op jit(solution)/shard_map/while/body/eval_jaxpr/psum | solution.py:9
  265.1 1.4 convolution_add_fusion.2
  266.4 1.6 select_select_fusion.2
  (2 shorter events, 0.0 us)
Async XLA Ops:
  6.5 1.6 copy-start
  6.5 67.7 %all-reduce.3.cloned.1.call-start = ((), (), s32[]{:S(2)}) async-start(), calls=%async_computation | async-start | bytes 2097152 | tf_op jit(solution)/shard_map/psum | solution.py:29
  75.8 44.6 %all-reduce.5.cloned.1.call-start = ((), (), s32[]{:S(2)}) async-start(), calls=%async_computation.1 | async-start | bytes 262144 | tf_op jit(solution)/shard_map/while/body/eval_jaxpr/psum | solution.py:9
  122.5 45.8 %all-reduce.5.cloned.1.call-start = ((), (), s32[]{:S(2)}) async-start(), calls=%async_computation.1 | async-start | bytes 262144 | tf_op jit(solution)/shard_map/while/body/eval_jaxpr/psum | solution.py:9
  171.2 45.5 %all-reduce.5.cloned.1.call-start = ((), (), s32[]{:S(2)}) async-start(), calls=%async_computation.1 | async-start | bytes 262144 | tf_op jit(solution)/shard_map/while/body/eval_jaxpr/psum | solution.py:9
  219.7 45.4 %all-reduce.5.cloned.1.call-start = ((), (), s32[]{:S(2)}) async-start(), calls=%async_computation.1 | async-start | bytes 262144 | tf_op jit(solution)/shard_map/while/body/eval_jaxpr/psum | solution.py:9
Sparse Core Ops, SparseCore 0:
  15.0 59.1 all-reduce.2
  79.5 40.8 all-reduce.4
  126.2 42.0 all-reduce.4
  174.6 42.0 all-reduce.4
  223.0 41.9 all-reduce.4
where the time goes:
time: 278 us; the launch traced here: 275 us
  waiting for transfers between devices  231 us (83%)
  matrix products  20 us (7%)
  between operations  13.1 us (5%)
  other arithmetic  9.23 us (3%)
    psum x4, waiting for transfers between devices, spread(): return lax.psum(block, axis)  173 us
    psum x1, waiting for transfers between devices, on_device(): summed = lax.psum(partial_value, 'col')  57.2 us
    dot_general x8, matrix products, precise_dot(): lax.dot_general(left, right, (((1,), (1,)), ((), ())), precision=lax.Prec...  13.2 us
    dot_general x1, matrix products, on_device(): lax.dot_general(prev_solution, prev_factor, (((1,), (1,)), ((), ())), pre...  6.77 us
  transfers between devices with their start and end apart: 5, of which 5 were waited for; matrix products, arithmetic and copies ran while one was open for 1% of the time, Pallas kernels for 0%

commit v1 on v0

v1 whole, which is shorter than its diff:
```python
import functools

import jax
import jax.numpy as jnp
from jax import lax
from jax.experimental import pallas as pl
from jax.experimental.pallas import tpu as pltpu
from jax.sharding import PartitionSpec as P

MESH = pl.DeviceIdType.MESH
CORES = 2
HALVES = 2


def dot_t(left, right):
    return lax.dot_general(
        left, right, (((1,), (1,)), ((), ())), preferred_element_type=jnp.float32
    )


def dot_split(left, right):
    high = left.astype(jnp.bfloat16)
    low = (left - high.astype(jnp.float32)).astype(jnp.bfloat16)
    return dot_t(high, right) + dot_t(low, right)


def kernel(
    n_row, n_col,
    z_hbm, pf_hbm, ps_hbm, sf_hbm, di_hbm,
    out_ref,
    z_v, pf, ps, sf, di, part, give, got, line, sol,
    load_sem, ps_sem, core_send, core_recv, line_send, line_recv, sol_send, sol_recv,
):
    n_z = n_col // CORES
    m, block = z_v.shape
    mh = m // HALVES
    row = lax.axis_index("row")
    col = lax.axis_index("col")
    p = col // CORES
    core = lax.rem(col, CORES)
    mate = col + 1 - 2 * core
    chunk = CORES * m
    low_half = p < n_z // 2

    barrier = pltpu.get_barrier_semaphore()

    def greet(device):
        pl.semaphore_signal(barrier, inc=1, device_id=device, device_id_type=MESH)

    greet({"col": mate})

    @pl.when(p > 0)
    def _():
        greet({"col": col - CORES})

    @pl.when(p < n_z - 1)
    def _():
        greet({"col": col + CORES})

    for other in range(n_row):
        @pl.when(row != other)
        def _():
            greet({"row": other})

    def target(i):
        return jnp.where(low_half, n_z - 1 - i, i)

    def ps_copy(i):
        rows = pl.ds(pl.multiple_of(target(i) * chunk, chunk), chunk)
        return pltpu.make_async_copy(ps_hbm.at[rows], ps.at[rows], ps_sem.at[i])

    pf_copy = pltpu.make_async_copy(pf_hbm, pf, load_sem.at[0])
    z_copy = pltpu.make_async_copy(z_hbm, z_v, load_sem.at[1])
    sf_copy = pltpu.make_async_copy(sf_hbm, sf, load_sem.at[2])
    di_copy = pltpu.make_async_copy(di_hbm, di, load_sem.at[3])
    pf_copy.start()
    for i in range(n_z):
        ps_copy(i).start()
    z_copy.start()
    sf_copy.start()
    di_copy.start()
    pf_copy.wait()

    def multiply(i):
        t = target(i)
        ps_copy(i).wait()
        rows = pl.multiple_of(t * chunk, chunk)
        theirs = ps[pl.ds(pl.multiple_of(rows + (1 - core) * m, m), m), :]
        give[t] = dot_t(theirs, pf[...])
        mine = ps[pl.ds(pl.multiple_of(rows + core * m, m), m), :]
        part[t] = dot_t(mine, pf[...])

    def core_copy(t):
        return pltpu.make_async_remote_copy(
            src_ref=give.at[t], dst_ref=got.at[t],
            send_sem=core_send.at[t], recv_sem=core_recv.at[t],
            device_id={"col": mate}, device_id_type=MESH,
        )

    def half(h):
        return pl.ds(h * mh, mh)

    def line_move(source, d, t, h):
        return pltpu.make_async_remote_copy(
            src_ref=source, dst_ref=line.at[d, t, half(h)],
            send_sem=line_send.at[d, t, h], recv_sem=line_recv.at[d, t, h],
            device_id={"col": col + CORES * (1 - 2 * d)}, device_id_type=MESH,
        )

    def pair_sum(i):
        t = target(i)
        core_copy(t).wait_recv()
        part[t] = part[t] + got[t]

        @pl.when((p == 0) & (t > 0))
        def _():
            for h in range(HALVES):
                line_move(part.at[t, half(h)], 0, t, h).start()

        @pl.when((p == n_z - 1) & (t < n_z - 1))
        def _():
            for h in range(HALVES):
                line_move(part.at[t, half(h)], 1, t, h).start()

    multiply(0)
    pl.semaphore_wait(
        barrier,
        n_row + (p > 0).astype(jnp.int32) + (p < n_z - 1).astype(jnp.int32),
    )
    core_copy(target(0)).start()

    @pl.loop(1, n_z)
    def _(i):
        multiply(i)
        core_copy(target(i)).start()
        pair_sum(i - 1)

    pair_sum(n_z - 1)

    first = jnp.where(low_half, 0, 1)
    inner = (p > 0) & (p < n_z - 1)

    @pl.loop(0, n_z - 1)
    def _(i):
        for e in range(2):
            d = first if e == 0 else 1 - first
            t = jnp.where(d == 0, n_z - 1 - i, i)

            @pl.when(inner & jnp.where(d == 0, t > p, t < p))
            def _():
                for h in range(HALVES):
                    line_move(line.at[d, t, half(h)], d, t, h).wait_recv()
                    line[d, t, half(h)] = line[d, t, half(h)] + part[t, half(h)]
                    line_move(line.at[d, t, half(h)], d, t, h).start()

    z_copy.wait()
    sf_copy.wait()
    di_copy.wait()

    def sol_copy(owner, h, to):
        return pltpu.make_async_remote_copy(
            src_ref=out_ref.at[half(h)], dst_ref=sol.at[owner, half(h)],
            send_sem=sol_send.at[to, h], recv_sem=sol_recv.at[owner, h],
            device_id={"row": to}, device_id_type=MESH,
        )

    for h in range(HALVES):
        part[p, half(h)] = z_v[half(h)] - part[p, half(h)]

        @pl.when(p > 0)
        def _():
            line_move(line.at[0, p, half(h)], 0, p, h).wait_recv()
            part[p, half(h)] = part[p, half(h)] - line[0, p, half(h)]

        @pl.when(p < n_z - 1)
        def _():
            line_move(line.at[1, p, half(h)], 1, p, h).wait_recv()
            part[p, half(h)] = part[p, half(h)] - line[1, p, half(h)]

        @pl.loop(0, row)
        def _(j):
            sol_copy(j, h, row).wait_recv()
            columns = pl.ds(pl.multiple_of(j * block, block), block)
            part[p, half(h)] = part[p, half(h)] - dot_split(sol[j, half(h)], sf[:, columns])

        out_ref[half(h)] = dot_split(part[p, half(h)], di[...])

        @pl.loop(row + 1, n_row)
        def _(j):
            sol_copy(row, h, j).start()

    for h in range(HALVES):
        @pl.loop(row + 1, n_row)
        def _(j):
            sol_copy(row, h, j).wait_send()

    @pl.loop(0, n_z)
    def _(t):
        core_copy(t).wait_send()
        for h in range(HALVES):
            @pl.when((p < n_z - 1) & (t > p))
            def _():
                line_move(line.at[0, t, half(h)], 0, t, h).wait_send()

            @pl.when((p > 0) & (t < p))
            def _():
                line_move(line.at[1, t, half(h)], 1, t, h).wait_send()


def on_device(n_row, n_col, z_slab, prev_factor, prev_solution, slab_factor, diag_inverse):
    m, block = z_slab.shape
    n_z = n_col // CORES
    anywhere = pl.BlockSpec(memory_space=pl.ANY)
    f32 = jnp.float32
    return pl.pallas_call(
        functools.partial(kernel, n_row, n_col),
        out_shape=jax.ShapeDtypeStruct((m, block), f32),
        in_specs=[anywhere] * 5,
        out_specs=pl.BlockSpec(memory_space=pltpu.VMEM),
        scratch_shapes=[
            pltpu.VMEM(z_slab.shape, f32),
            pltpu.VMEM(prev_factor.shape, prev_factor.dtype),
            pltpu.VMEM(prev_solution.shape, prev_solution.dtype),
            pltpu.VMEM(slab_factor.shape, slab_factor.dtype),
            pltpu.VMEM(diag_inverse.shape, diag_inverse.dtype),
            pltpu.VMEM((n_z, m, block), f32),
            pltpu.VMEM((n_z, m, block), f32),
            pltpu.VMEM((n_z, m, block), f32),
            pltpu.VMEM((2, n_z, m, block), f32),
            pltpu.VMEM((n_row, m, block), f32),
            pltpu.SemaphoreType.DMA((4,)),
            pltpu.SemaphoreType.DMA((n_z,)),
            pltpu.SemaphoreType.DMA((n_z,)),
            pltpu.SemaphoreType.DMA((n_z,)),
            pltpu.SemaphoreType.DMA((2, n_z, HALVES)),
            pltpu.SemaphoreType.DMA((2, n_z, HALVES)),
            pltpu.SemaphoreType.DMA((n_row, HALVES)),
            pltpu.SemaphoreType.DMA((n_row, HALVES)),
        ],
        compiler_params=pltpu.CompilerParams(
            collective_id=0, has_side_effects=True, vmem_limit_bytes=40 * 2**20
        ),
    )(z_slab, prev_factor, prev_solution, slab_factor, diag_inverse)


def solution(mesh):
    in_specs = (P("col", "row"), P("row", "col"), P(None, "col"), P("row", None), P("row", None))
    return jax.shard_map(
        functools.partial(on_device, mesh.shape["row"], mesh.shape["col"]),
        mesh=mesh, in_specs=in_specs, out_specs=P("col", "row"), check_vma=False,
    )
```

time: 278 us -> 39.5 us (0.14); the launches traced: 275 us -> 39.2 us
  waiting for transfers between devices: 231 us -> 0 us
  Pallas kernels: 0 us -> 30.7 us
  matrix products: 20 us -> 0 us
  between operations: 13.1 us -> 0.01 us
  other arithmetic: 9.23 us -> 0 us
  local copies, waits for them, and re-layouts: 1.59 us -> 8.48 us
    psum x5 -> x0, waiting for transfers between devices: 230 us -> none  [the longest x4 173 us: spread(): return lax.psum(block, axis)]
    pallas_call x0 -> x1, Pallas kernels: none -> 30.7 us  [on_device(): pl.pallas_call(functools.partial(kernel, n_row, n_col), out_shape=jax.Sha...]
    dot_general x9 -> x0, matrix products: 20 us -> none  [the longest x8 13.2 us: precise_dot(): lax.dot_general(left, right, (((1,), (1,)), ((), ())), precision=lax.Prec...]
    unnamed x2 -> x11, local copies, waits for them, and re-layouts: 1.59 us -> 8.48 us
    select_n x4 -> x0, other arithmetic: 5.52 us -> none  [bcast_step(): result = jnp.where(device_row == block_index, arrived, result)]
  transfers between devices with their start and end apart: 5 -> 0, of which waited for: 5 -> 0; matrix products, arithmetic and copies ran while one was open for 1% -> 0% of each run, Pallas kernels for 0% -> 0%
where the time goes in v1:
time: 39.5 us; the launch traced here: 39.2 us
  Pallas kernels  30.7 us (78%)
  local copies, waits for them, and re-layouts  8.48 us (21%)
    pallas_call x1, Pallas kernels, on_device(): pl.pallas_call(functools.partial(kernel, n_row, n_col), out_shape=jax.Sha...  30.7 us
    unnamed x11, local copies, waits for them, and re-layouts  8.48 us

profile of v1, /device:TPU:14, one launch (start us, length us, event | category | flops | bytes accessed | tf_op | source)
XLA Modules:
  0.0 39.2 jit_solution(5232897809669624854)
XLA Ops:
  0.0 0.0 copy-start
  0.0 3.4 %copy-done = bf16[1024,4096]{1,0:T(8,128)(2,1)S(1)} copy-done((bf16[1024,4096]{1,0:T(8,128)(2,1)S(1)}, bf16[1024,4096]{1,0:T(8,128)(2,1)}, u32[]{:S(2)}) %copy-start) | copy-done | bytes 8388632
  3.4 0.0 copy-start.1
  3.4 1.6 %copy-done.1 = bf16[256,4096]{1,0:T(8,128)(2,1)S(1)} copy-done((bf16[256,4096]{1,0:T(8,128)(2,1)S(1)}, bf16[256,4096]{1,0:T(8,128)(2,1)}, u32[]{:S(2)}) %copy-start.1) | copy-done | bytes 2097176
  5.0 0.0 copy-start.2
  5.0 1.0 %copy-done.2 = bf16[256,1024]{1,0:T(8,128)(2,1)S(1)} copy-done((bf16[256,1024]{1,0:T(8,128)(2,1)S(1)}, bf16[256,1024]{1,0:T(8,128)(2,1)}, u32[]{:S(2)}) %copy-start.2) | copy-done | bytes 524312
  6.0 0.0 copy-start.3
  6.0 0.9 %copy-done.3 = f32[128,256]{1,0:T(8,128)S(1)} copy-done((f32[128,256]{1,0:T(8,128)S(1)}, f32[128,256]{1,0:T(8,128)}, u32[]{:S(2)}) %copy-start.3) | copy-done | bytes 131096
  6.9 0.0 copy-start.4
  6.9 0.9 %copy-done.4 = bf16[256,256]{1,0:T(8,128)(2,1)S(1)} copy-done((bf16[256,256]{1,0:T(8,128)(2,1)S(1)}, bf16[256,256]{1,0:T(8,128)(2,1)}, u32[]{:S(2)}) %copy-start.4) | copy-done | bytes 131096
  7.8 30.7 %shard_map.55 = f32[128,256]{1,0:T(8,128)S(1)} custom-call(f32[128,256]{1,0:T(8,128)S(1)} %copy-done.3, bf16[256,4096]{1,0:T(8,128)(2,1)S(1)} %copy-done.1, bf16[1024,4096]{1,0:T(8,128)(2,1)S(1)} %copy-done, bf16[256,1024]{1,0:T(8,128)(2,1)S(1)} %copy-done.2, bf16[256,256]{1,0:T(8,128)(2,1)S(1)} %copy-done.4), custom_call_target="tpu_custom_call" | custom-call | tf_op jit(solution)/shard_map/pallas_call | solution.py:215
  38.6 0.7 %copy.7 = f32[128,256]{1,0:T(8,128)} copy(f32[128,256]{1,0:T(8,128)S(1)} %shard_map.55) | data formatting | bytes 262144
Async XLA Ops:
  0.0 3.4 %copy-start = (bf16[1024,4096]{1,0:T(8,128)(2,1)S(1)}, bf16[1024,4096]{1,0:T(8,128)(2,1)}, u32[]{:S(2)}) copy-start(bf16[1024,4096]{1,0:T(8,128)(2,1)} %ps_hbm.1) | copy-start | bytes 25165828
  3.4 1.6 %copy-start.1 = (bf16[256,4096]{1,0:T(8,128)(2,1)S(1)}, bf16[256,4096]{1,0:T(8,128)(2,1)}, u32[]{:S(2)}) copy-start(bf16[256,4096]{1,0:T(8,128)(2,1)} %pf_hbm.1) | copy-start | bytes 6291460
  5.0 1.0 %copy-start.2 = (bf16[256,1024]{1,0:T(8,128)(2,1)S(1)}, bf16[256,1024]{1,0:T(8,128)(2,1)}, u32[]{:S(2)}) copy-start(bf16[256,1024]{1,0:T(8,128)(2,1)} %sf_hbm.1) | copy-start | bytes 1572868
  6.0 0.9 %copy-start.3 = (f32[128,256]{1,0:T(8,128)S(1)}, f32[128,256]{1,0:T(8,128)}, u32[]{:S(2)}) copy-start(f32[128,256]{1,0:T(8,128)} %z_hbm.1) | copy-start | bytes 393220
  6.9 0.9 %copy-start.4 = (bf16[256,256]{1,0:T(8,128)(2,1)S(1)}, bf16[256,256]{1,0:T(8,128)(2,1)}, u32[]{:S(2)}) copy-start(bf16[256,256]{1,0:T(8,128)(2,1)} %di_hbm.1) | copy-start | bytes 393220

commit v2 on v1

--- a/solution.py
+++ b/solution.py
@@ -9,7 +9,8 @@
 
 MESH = pl.DeviceIdType.MESH
 CORES = 2
-HALVES = 2
+HALVES = 4
+GATHER_ROWS = 4
 
 
 def dot_t(left, right):
@@ -22,6 +23,15 @@
     high = left.astype(jnp.bfloat16)
     low = (left - high.astype(jnp.float32)).astype(jnp.bfloat16)
     return dot_t(high, right) + dot_t(low, right)
+
+
+def dot_n(left, right):
+    return jnp.dot(left, right, preferred_element_type=jnp.float32)
+
+
+def split(value):
+    high = value.astype(jnp.bfloat16)
+    return high, (value - high.astype(jnp.float32)).astype(jnp.bfloat16)
 
 
 def kernel(
@@ -30,7 +40,9 @@
     out_ref,
     z_v, pf, ps, sf, di, part, give, got, line, sol,
     load_sem, ps_sem, core_send, core_recv, line_send, line_recv, sol_send, sol_recv,
+    raw, coef, g_high, g_low, raw_send, raw_recv, pair_send, pair_recv,
 ):
+    gathered = n_row <= GATHER_ROWS
     n_z = n_col // CORES
     m, block = z_v.shape
     mh = m // HALVES
@@ -73,13 +85,52 @@
     z_copy = pltpu.make_async_copy(z_hbm, z_v, load_sem.at[1])
     sf_copy = pltpu.make_async_copy(sf_hbm, sf, load_sem.at[2])
     di_copy = pltpu.make_async_copy(di_hbm, di, load_sem.at[3])
+    sf_copy.start()
+    di_copy.start()
     pf_copy.start()
     for i in range(n_z):
         ps_copy(i).start()
     z_copy.start()
-    sf_copy.start()
-    di_copy.start()
+
+    b_half = block // 2
+    own_half = pl.ds(pl.multiple_of(core * b_half, b_half), b_half)
+
+    def raw_copy(i, j, to):
+        return pltpu.make_async_remote_copy(
+            src_ref=raw.at[i, j, own_half], dst_ref=raw.at[i, j, own_half],
+            send_sem=raw_send.at[to, j], recv_sem=raw_recv.at[i, j],
+            device_id={"row": to}, device_id_type=MESH,
+        )
+
+    def pair_copy(i, j):
+        return pltpu.make_async_remote_copy(
+            src_ref=raw.at[i, j, own_half], dst_ref=raw.at[i, j, own_half],
+            send_sem=pair_send.at[i, j], recv_sem=pair_recv.at[i, j],
+            device_id={"col": mate}, device_id_type=MESH,
+        )
+
+    def columns_of(j):
+        return pl.ds(pl.multiple_of(j * block, block), block)
+
+    sf_copy.wait()
+    di_copy.wait()
+    if gathered:
+        @pl.when(row < n_row - 1)
+        def _():
+            raw[row, row, own_half] = di[own_half].astype(jnp.float32)
+
+            @pl.loop(0, row)
+            def _(j):
+                raw[row, j, own_half] = sf[own_half, columns_of(j)].astype(jnp.float32)
+
     pf_copy.wait()
+
+    def core_copy(t):
+        return pltpu.make_async_remote_copy(
+            src_ref=give.at[t], dst_ref=got.at[t],
+            send_sem=core_send.at[t], recv_sem=core_recv.at[t],
+            device_id={"col": mate}, device_id_type=MESH,
+        )
 
     def multiply(i):
         t = target(i)
@@ -87,15 +138,14 @@
         rows = pl.multiple_of(t * chunk, chunk)
         theirs = ps[pl.ds(pl.multiple_of(rows + (1 - core) * m, m), m), :]
         give[t] = dot_t(theirs, pf[...])
+        if isinstance(i, int):
+            pl.semaphore_wait(
+                barrier,
+                n_row + (p > 0).astype(jnp.int32) + (p < n_z - 1).astype(jnp.int32),
+            )
+        core_copy(t).start()
         mine = ps[pl.ds(pl.multiple_of(rows + core * m, m), m), :]
         part[t] = dot_t(mine, pf[...])
-
-    def core_copy(t):
-        return pltpu.make_async_remote_copy(
-            src_ref=give.at[t], dst_ref=got.at[t],
-            send_sem=core_send.at[t], recv_sem=core_recv.at[t],
-            device_id={"col": mate}, device_id_type=MESH,
-        )
 
     def half(h):
         return pl.ds(h * mh, mh)
@@ -123,16 +173,16 @@
                 line_move(part.at[t, half(h)], 1, t, h).start()
 
     multiply(0)
-    pl.semaphore_wait(
-        barrier,
-        n_row + (p > 0).astype(jnp.int32) + (p < n_z - 1).astype(jnp.int32),
-    )
-    core_copy(target(0)).start()
+    if gathered:
+        @pl.loop(row + 1, n_row)
+        def _(to):
+            @pl.loop(0, row + 1)
+            def _(j):
+                raw_copy(row, j, to).start()
 
     @pl.loop(1, n_z)
     def _(i):
         multiply(i)
-        core_copy(target(i)).start()
         pair_sum(i - 1)
 
     pair_sum(n_z - 1)
@@ -154,17 +204,50 @@
                     line_move(line.at[d, t, half(h)], d, t, h).start()
 
     z_copy.wait()
-    sf_copy.wait()
-    di_copy.wait()
+    if gathered:
+        @pl.loop(0, row)
+        def _(k):
+            i = row - 1 - k
+
+            @pl.loop(0, i + 1)
+            def _(j):
+                raw_copy(i, j, row).wait_recv()
+                pair_copy(i, j).start()
+
+        @pl.loop(0, row)
+        def _(j):
+            coef[j] = -dot_n(di[...], sf[:, columns_of(j)])
+
+        @pl.loop(0, row)
+        def _(k):
+            j = row - 1 - k
+            high, low = split(coef[j])
+            pair_copy(j, j).wait_recv()
+            inverse = raw[j, j].astype(jnp.bfloat16)
+            high, low = split(dot_n(high, inverse) + dot_n(low, inverse))
+            g_high[j] = high
+            g_low[j] = low
+
+            @pl.loop(0, j)
+            def _(i):
+                pair_copy(j, i).wait_recv()
+                factor = raw[j, i].astype(jnp.bfloat16)
+                coef[i] = coef[i] - dot_n(g_high[j], factor) - dot_n(g_low[j], factor)
 
     def sol_copy(owner, h, to):
-        return pltpu.make_async_remote_copy(
-            src_ref=out_ref.at[half(h)], dst_ref=sol.at[owner, half(h)],
+        source = part.at[p, half(h)] if gathered else out_ref.at[half(h)]
+        return pltpu.make_async_remote_copy(
+            src_ref=source, dst_ref=sol.at[owner, half(h)],
             send_sem=sol_send.at[to, h], recv_sem=sol_recv.at[owner, h],
             device_id={"row": to}, device_id_type=MESH,
         )
 
-    for h in range(HALVES):
+    def send_on(h):
+        @pl.loop(row + 1, n_row)
+        def _(j):
+            sol_copy(row, h, j).start()
+
+    def finish_sum(h):
         part[p, half(h)] = z_v[half(h)] - part[p, half(h)]
 
         @pl.when(p > 0)
@@ -177,17 +260,49 @@
             line_move(line.at[1, p, half(h)], 1, p, h).wait_recv()
             part[p, half(h)] = part[p, half(h)] - line[1, p, half(h)]
 
+    def apply_rows(h):
+        out_ref[half(h)] = dot_split(part[p, half(h)], di[...])
+
         @pl.loop(0, row)
         def _(j):
             sol_copy(j, h, row).wait_recv()
-            columns = pl.ds(pl.multiple_of(j * block, block), block)
-            part[p, half(h)] = part[p, half(h)] - dot_split(sol[j, half(h)], sf[:, columns])
+            high, low = split(sol[j, half(h)])
+            out_ref[half(h)] = out_ref[half(h)] + (
+                dot_t(high, g_high[j]) + dot_t(low, g_high[j]) + dot_t(high, g_low[j])
+            )
+
+    def chain_rows(h):
+        @pl.loop(0, row)
+        def _(j):
+            sol_copy(j, h, row).wait_recv()
+            part[p, half(h)] = part[p, half(h)] - dot_split(sol[j, half(h)], sf[:, columns_of(j)])
 
         out_ref[half(h)] = dot_split(part[p, half(h)], di[...])
+        send_on(h)
+
+    if gathered:
+        for h in range(HALVES + 1):
+            if h < HALVES:
+                finish_sum(h)
+                send_on(h)
+            if h > 0:
+                apply_rows(h - 1)
 
         @pl.loop(row + 1, n_row)
-        def _(j):
-            sol_copy(row, h, j).start()
+        def _(to):
+            @pl.loop(0, row + 1)
+            def _(j):
+                raw_copy(row, j, to).wait_send()
+
+        @pl.loop(0, row)
+        def _(i):
+            @pl.loop(0, i + 1)
+            def _(j):
+                pair_copy(i, j).wait_send()
+    else:
+        for h in range(HALVES):
+            finish_sum(h)
+            chain_rows(h)
 
     for h in range(HALVES):
         @pl.loop(row + 1, n_row)
@@ -210,8 +325,9 @@
 def on_device(n_row, n_col, z_slab, prev_factor, prev_solution, slab_factor, diag_inverse):
     m, block = z_slab.shape
     n_z = n_col // CORES
-    anywhere = pl.BlockSpec(memory_space=pl.ANY)
+    anywhere = pl.BlockSpec(memory_space=pltpu.HBM)
     f32 = jnp.float32
+    held = n_row if n_row <= GATHER_ROWS else 1
     return pl.pallas_call(
         functools.partial(kernel, n_row, n_col),
         out_shape=jax.ShapeDtypeStruct((m, block), f32),
@@ -236,9 +352,17 @@
             pltpu.SemaphoreType.DMA((2, n_z, HALVES)),
             pltpu.SemaphoreType.DMA((n_row, HALVES)),
             pltpu.SemaphoreType.DMA((n_row, HALVES)),
+            pltpu.VMEM((held, held, block, block), f32),
+            pltpu.VMEM((held, block, block), f32),
+            pltpu.VMEM((held, block, block), jnp.bfloat16),
+            pltpu.VMEM((held, block, block), jnp.bfloat16),
+            pltpu.SemaphoreType.DMA((held, held)),
+            pltpu.SemaphoreType.DMA((held, held)),
+            pltpu.SemaphoreType.DMA((held, held)),
+            pltpu.SemaphoreType.DMA((held, held)),
         ],
         compiler_params=pltpu.CompilerParams(
-            collective_id=0, has_side_effects=True, vmem_limit_bytes=40 * 2**20
+            collective_id=0, has_side_effects=True, vmem_limit_bytes=60 * 2**20
         ),
     )(z_slab, prev_factor, prev_solution, slab_factor, diag_inverse)
 

time: 39.5 us -> 32.4 us (0.82)
  local copies, waits for them, and re-layouts: 8.48 us -> 1.57 us
    unnamed x11 -> x1, local copies, waits for them, and re-layouts: 8.48 us -> 1.57 us
where the time goes in v2:
time: 32.4 us; the launch traced here: 32.2 us
  Pallas kernels  30.7 us (95%)
  local copies, waits for them, and re-layouts  1.57 us (5%)
    pallas_call x1, Pallas kernels, on_device(): pl.pallas_call(functools.partial(kernel, n_row, n_col), out_shape=jax.Sha...  30.7 us
    unnamed x1, local copies, waits for them, and re-layouts  1.57 us

profile of v2, /device:TPU:14, one launch (start us, length us, event | category | flops | bytes accessed | tf_op | source)
XLA Modules:
  0.0 32.2 jit_solution(13692406071365374506)
XLA Ops:
  0.0 30.7 %shard_map.55 = f32[128,256]{1,0:T(8,128)} custom-call(f32[128,256]{1,0:T(8,128)} %z_hbm.1, bf16[256,4096]{1,0:T(8,128)(2,1)} %pf_hbm.1, bf16[1024,4096]{1,0:T(8,128)(2,1)} %ps_hbm.1, bf16[256,1024]{1,0:T(8,128)(2,1)} %sf_hbm.1, bf16[256,256]{1,0:T(8,128)(2,1)} %di_hbm.1), custom_call_target="tpu_custom_call" | custom-call | tf_op jit(solution)/shard_map/pallas_call | solution.py:331
  30.7 1.6 %copy.7 = f32[128,256]{1,0:T(8,128)} copy(f32[128,256]{1,0:T(8,128)} %shard_map.55) | data formatting | bytes 262144

commit v3 on v2

--- a/solution.py
+++ b/solution.py
@@ -9,7 +9,7 @@
 
 MESH = pl.DeviceIdType.MESH
 CORES = 2
-HALVES = 4
+HALVES = 2
 GATHER_ROWS = 4
 
 
@@ -40,7 +40,7 @@
     out_ref,
     z_v, pf, ps, sf, di, part, give, got, line, sol,
     load_sem, ps_sem, core_send, core_recv, line_send, line_recv, sol_send, sol_recv,
-    raw, coef, g_high, g_low, raw_send, raw_recv, pair_send, pair_recv,
+    pf_t, raw, coef, g_high, g_low, raw_send, raw_recv, pair_send, pair_recv,
 ):
     gathered = n_row <= GATHER_ROWS
     n_z = n_col // CORES
@@ -124,6 +124,7 @@
                 raw[row, j, own_half] = sf[own_half, columns_of(j)].astype(jnp.float32)
 
     pf_copy.wait()
+    pf_t[...] = pf[...].T
 
     def core_copy(t):
         return pltpu.make_async_remote_copy(
@@ -137,7 +138,7 @@
         ps_copy(i).wait()
         rows = pl.multiple_of(t * chunk, chunk)
         theirs = ps[pl.ds(pl.multiple_of(rows + (1 - core) * m, m), m), :]
-        give[t] = dot_t(theirs, pf[...])
+        give[t] = dot_n(theirs, pf_t[...])
         if isinstance(i, int):
             pl.semaphore_wait(
                 barrier,
@@ -145,7 +146,7 @@
             )
         core_copy(t).start()
         mine = ps[pl.ds(pl.multiple_of(rows + core * m, m), m), :]
-        part[t] = dot_t(mine, pf[...])
+        part[t] = dot_n(mine, pf_t[...])
 
     def half(h):
         return pl.ds(h * mh, mh)
@@ -214,6 +215,20 @@
                 raw_copy(i, j, row).wait_recv()
                 pair_copy(i, j).start()
 
+        def set_rows(j, value):
+            rows = columns_of(j)
+            high, low = split(value.T)
+            g_high[rows] = high
+            g_low[rows] = low
+
+        set_rows(row, di[...].astype(jnp.float32))
+
+        @pl.loop(row + 1, n_row)
+        def _(j):
+            g_high[columns_of(j)] = jnp.zeros((block, block), jnp.bfloat16)
+            g_low[columns_of(j)] = jnp.zeros((block, block), jnp.bfloat16)
+            sol[j] = jnp.zeros((m, block), jnp.float32)
+
         @pl.loop(0, row)
         def _(j):
             coef[j] = -dot_n(di[...], sf[:, columns_of(j)])
@@ -224,18 +239,18 @@
             high, low = split(coef[j])
             pair_copy(j, j).wait_recv()
             inverse = raw[j, j].astype(jnp.bfloat16)
-            high, low = split(dot_n(high, inverse) + dot_n(low, inverse))
-            g_high[j] = high
-            g_low[j] = low
+            composed = dot_n(high, inverse) + dot_n(low, inverse)
+            set_rows(j, composed)
+            high, low = split(composed)
 
             @pl.loop(0, j)
             def _(i):
                 pair_copy(j, i).wait_recv()
                 factor = raw[j, i].astype(jnp.bfloat16)
-                coef[i] = coef[i] - dot_n(g_high[j], factor) - dot_n(g_low[j], factor)
+                coef[i] = coef[i] - dot_n(high, factor) - dot_n(low, factor)
 
     def sol_copy(owner, h, to):
-        source = part.at[p, half(h)] if gathered else out_ref.at[half(h)]
+        source = sol.at[row, half(h)] if gathered else out_ref.at[half(h)]
         return pltpu.make_async_remote_copy(
             src_ref=source, dst_ref=sol.at[owner, half(h)],
             send_sem=sol_send.at[to, h], recv_sem=sol_recv.at[owner, h],
@@ -261,15 +276,14 @@
             part[p, half(h)] = part[p, half(h)] - line[1, p, half(h)]
 
     def apply_rows(h):
-        out_ref[half(h)] = dot_split(part[p, half(h)], di[...])
-
         @pl.loop(0, row)
         def _(j):
             sol_copy(j, h, row).wait_recv()
-            high, low = split(sol[j, half(h)])
-            out_ref[half(h)] = out_ref[half(h)] + (
-                dot_t(high, g_high[j]) + dot_t(low, g_high[j]) + dot_t(high, g_low[j])
-            )
+
+        remainders = jnp.concatenate([sol[j, half(h)] for j in range(n_row)], axis=1)
+        high, low = split(remainders)
+        both = dot_n(jnp.concatenate([high, low], axis=0), g_high[...])
+        out_ref[half(h)] = both[:mh] + both[mh:] + dot_n(high, g_low[...])
 
     def chain_rows(h):
         @pl.loop(0, row)
@@ -284,6 +298,7 @@
         for h in range(HALVES + 1):
             if h < HALVES:
                 finish_sum(h)
+                sol[row, half(h)] = part[p, half(h)]
                 send_on(h)
             if h > 0:
                 apply_rows(h - 1)
@@ -352,10 +367,11 @@
             pltpu.SemaphoreType.DMA((2, n_z, HALVES)),
             pltpu.SemaphoreType.DMA((n_row, HALVES)),
             pltpu.SemaphoreType.DMA((n_row, HALVES)),
+            pltpu.VMEM(prev_factor.shape[::-1], prev_factor.dtype),
             pltpu.VMEM((held, held, block, block), f32),
             pltpu.VMEM((held, block, block), f32),
-            pltpu.VMEM((held, block, block), jnp.bfloat16),
-            pltpu.VMEM((held, block, block), jnp.bfloat16),
+            pltpu.VMEM((held * block, block), jnp.bfloat16),
+            pltpu.VMEM((held * block, block), jnp.bfloat16),
             pltpu.SemaphoreType.DMA((held, held)),
             pltpu.SemaphoreType.DMA((held, held)),
             pltpu.SemaphoreType.DMA((held, held)),

time: 32.4 us -> 28.7 us (0.89)
  Pallas kernels: 30.7 us -> 26.9 us
    pallas_call x1, Pallas kernels: 30.7 us -> 26.9 us  [on_device(): pl.pallas_call(functools.partial(kernel, n_row, n_col), out_shape=jax.Sha...]
where the time goes in v3:
time: 28.7 us; the launch traced here: 28.4 us
  Pallas kernels  26.9 us (94%)
  local copies, waits for them, and re-layouts  1.57 us (5%)
    pallas_call x1, Pallas kernels, on_device(): pl.pallas_call(functools.partial(kernel, n_row, n_col), out_shape=jax.Sha...  26.9 us
    unnamed x1, local copies, waits for them, and re-layouts  1.57 us

profile of v3, /device:TPU:14, one launch (start us, length us, event | category | flops | bytes accessed | tf_op | source)
XLA Modules:
  0.0 28.4 jit_solution(2457212493813970358)
XLA Ops:
  0.0 26.9 %shard_map.55 = f32[128,256]{1,0:T(8,128)} custom-call(f32[128,256]{1,0:T(8,128)} %z_hbm.1, bf16[256,4096]{1,0:T(8,128)(2,1)} %pf_hbm.1, bf16[1024,4096]{1,0:T(8,128)(2,1)} %ps_hbm.1, bf16[256,1024]{1,0:T(8,128)(2,1)} %sf_hbm.1, bf16[256,256]{1,0:T(8,128)(2,1)} %di_hbm.1), custom_call_target="tpu_custom_call" | custom-call | tf_op jit(solution)/shard_map/pallas_call | solution.py:346
  26.9 1.6 %copy.7 = f32[128,256]{1,0:T(8,128)} copy(f32[128,256]{1,0:T(8,128)} %shard_map.55) | data formatting | bytes 262144

commit v4 on v3

--- a/solution.py
+++ b/solution.py
@@ -85,10 +85,11 @@
     z_copy = pltpu.make_async_copy(z_hbm, z_v, load_sem.at[1])
     sf_copy = pltpu.make_async_copy(sf_hbm, sf, load_sem.at[2])
     di_copy = pltpu.make_async_copy(di_hbm, di, load_sem.at[3])
+    pf_copy.start()
+    ps_copy(0).start()
     sf_copy.start()
     di_copy.start()
-    pf_copy.start()
-    for i in range(n_z):
+    for i in range(1, n_z):
         ps_copy(i).start()
     z_copy.start()
 
@@ -111,17 +112,6 @@
 
     def columns_of(j):
         return pl.ds(pl.multiple_of(j * block, block), block)
-
-    sf_copy.wait()
-    di_copy.wait()
-    if gathered:
-        @pl.when(row < n_row - 1)
-        def _():
-            raw[row, row, own_half] = di[own_half].astype(jnp.float32)
-
-            @pl.loop(0, row)
-            def _(j):
-                raw[row, j, own_half] = sf[own_half, columns_of(j)].astype(jnp.float32)
 
     pf_copy.wait()
     pf_t[...] = pf[...].T
@@ -174,19 +164,30 @@
                 line_move(part.at[t, half(h)], 1, t, h).start()
 
     multiply(0)
+    sf_copy.wait()
+    di_copy.wait()
+    if gathered:
+        @pl.when(row < n_row - 1)
+        def _():
+            raw[row, row, own_half] = di[own_half].astype(jnp.float32)
+
+            @pl.loop(0, row)
+            def _(j):
+                raw[row, j, own_half] = sf[own_half, columns_of(j)].astype(jnp.float32)
+
     if gathered:
         @pl.loop(row + 1, n_row)
         def _(to):
             @pl.loop(0, row + 1)
             def _(j):
                 raw_copy(row, j, to).start()
+
+    pair_sum(0)
 
     @pl.loop(1, n_z)
     def _(i):
         multiply(i)
-        pair_sum(i - 1)
-
-    pair_sum(n_z - 1)
+        pair_sum(i)
 
     first = jnp.where(low_half, 0, 1)
     inner = (p > 0) & (p < n_z - 1)

time: 28.7 us -> 27.7 us (0.965)
  Pallas kernels: 26.9 us -> 25.9 us
    pallas_call x1, Pallas kernels: 26.9 us -> 25.9 us  [on_device(): pl.pallas_call(functools.partial(kernel, n_row, n_col), out_shape=jax.Sha...]
where the time goes in v4:
time: 27.7 us; the launch traced here: 27.5 us
  Pallas kernels  25.9 us (94%)
  local copies, waits for them, and re-layouts  1.57 us (6%)
    pallas_call x1, Pallas kernels, on_device(): pl.pallas_call(functools.partial(kernel, n_row, n_col), out_shape=jax.Sha...  25.9 us
    unnamed x1, local copies, waits for them, and re-layouts  1.57 us

profile of v4, /device:TPU:14, one launch (start us, length us, event | category | flops | bytes accessed | tf_op | source)
XLA Modules:
  0.0 27.5 jit_solution(12211336692005487225)
XLA Ops:
  0.0 25.9 %shard_map.55 = f32[128,256]{1,0:T(8,128)} custom-call(f32[128,256]{1,0:T(8,128)} %z_hbm.1, bf16[256,4096]{1,0:T(8,128)(2,1)} %pf_hbm.1, bf16[1024,4096]{1,0:T(8,128)(2,1)} %ps_hbm.1, bf16[256,1024]{1,0:T(8,128)(2,1)} %sf_hbm.1, bf16[256,256]{1,0:T(8,128)(2,1)} %di_hbm.1), custom_call_target="tpu_custom_call" | custom-call | tf_op jit(solution)/shard_map/pallas_call | solution.py:347
  25.9 1.6 %copy.7 = f32[128,256]{1,0:T(8,128)} copy(f32[128,256]{1,0:T(8,128)} %shard_map.55) | data formatting | bytes 262144

commit v5 on v4

--- a/solution.py
+++ b/solution.py
@@ -116,10 +116,10 @@
     pf_copy.wait()
     pf_t[...] = pf[...].T
 
-    def core_copy(t):
-        return pltpu.make_async_remote_copy(
-            src_ref=give.at[t], dst_ref=got.at[t],
-            send_sem=core_send.at[t], recv_sem=core_recv.at[t],
+    def core_copy(t, h):
+        return pltpu.make_async_remote_copy(
+            src_ref=give.at[t, half(h)], dst_ref=got.at[t, half(h)],
+            send_sem=core_send.at[t, h], recv_sem=core_recv.at[t, h],
             device_id={"col": mate}, device_id_type=MESH,
         )
 
@@ -134,7 +134,8 @@
                 barrier,
                 n_row + (p > 0).astype(jnp.int32) + (p < n_z - 1).astype(jnp.int32),
             )
-        core_copy(t).start()
+        for h in range(HALVES):
+            core_copy(t, h).start()
         mine = ps[pl.ds(pl.multiple_of(rows + core * m, m), m), :]
         part[t] = dot_n(mine, pf_t[...])
 
@@ -150,17 +151,16 @@
 
     def pair_sum(i):
         t = target(i)
-        core_copy(t).wait_recv()
-        part[t] = part[t] + got[t]
-
-        @pl.when((p == 0) & (t > 0))
-        def _():
-            for h in range(HALVES):
+        for h in range(HALVES):
+            core_copy(t, h).wait_recv()
+            part[t, half(h)] = part[t, half(h)] + got[t, half(h)]
+
+            @pl.when((p == 0) & (t > 0))
+            def _():
                 line_move(part.at[t, half(h)], 0, t, h).start()
 
-        @pl.when((p == n_z - 1) & (t < n_z - 1))
-        def _():
-            for h in range(HALVES):
+            @pl.when((p == n_z - 1) & (t < n_z - 1))
+            def _():
                 line_move(part.at[t, half(h)], 1, t, h).start()
 
     multiply(0)
@@ -327,8 +327,9 @@
 
     @pl.loop(0, n_z)
     def _(t):
-        core_copy(t).wait_send()
         for h in range(HALVES):
+            core_copy(t, h).wait_send()
+
             @pl.when((p < n_z - 1) & (t > p))
             def _():
                 line_move(line.at[0, t, half(h)], 0, t, h).wait_send()
@@ -362,8 +363,8 @@
             pltpu.VMEM((n_row, m, block), f32),
             pltpu.SemaphoreType.DMA((4,)),
             pltpu.SemaphoreType.DMA((n_z,)),
-            pltpu.SemaphoreType.DMA((n_z,)),
-            pltpu.SemaphoreType.DMA((n_z,)),
+            pltpu.SemaphoreType.DMA((n_z, HALVES)),
+            pltpu.SemaphoreType.DMA((n_z, HALVES)),
             pltpu.SemaphoreType.DMA((2, n_z, HALVES)),
             pltpu.SemaphoreType.DMA((2, n_z, HALVES)),
             pltpu.SemaphoreType.DMA((n_row, HALVES)),

time: 27.7 us -> 27.7 us (level)
  no operation moved by 1% of the time
where the time goes in v5:
time: 27.7 us; the launch traced here: 27.5 us
  Pallas kernels  25.9 us (94%)
  local copies, waits for them, and re-layouts  1.57 us (6%)
    pallas_call x1, Pallas kernels, on_device(): pl.pallas_call(functools.partial(kernel, n_row, n_col), out_shape=jax.Sha...  25.9 us
    unnamed x1, local copies, waits for them, and re-layouts  1.57 us

profile of v5, /device:TPU:14, one launch (start us, length us, event | category | flops | bytes accessed | tf_op | source)
XLA Modules:
  0.0 27.5 jit_solution(15176561326815827450)
XLA Ops:
  0.0 25.9 %shard_map.55 = f32[128,256]{1,0:T(8,128)} custom-call(f32[128,256]{1,0:T(8,128)} %z_hbm.1, bf16[256,4096]{1,0:T(8,128)(2,1)} %pf_hbm.1, bf16[1024,4096]{1,0:T(8,128)(2,1)} %ps_hbm.1, bf16[256,1024]{1,0:T(8,128)(2,1)} %sf_hbm.1, bf16[256,256]{1,0:T(8,128)(2,1)} %di_hbm.1), custom_call_target="tpu_custom_call" | custom-call | tf_op jit(solution)/shard_map/pallas_call | solution.py:348
  25.9 1.6 %copy.7 = f32[128,256]{1,0:T(8,128)} copy(f32[128,256]{1,0:T(8,128)} %shard_map.55) | data formatting | bytes 262144
